TPU v7x, 32 devices: a whole 2x2x4 slice. The times are simulated.
32 devices in a mesh: row: 8 (over z, x), col: 4 (over y, core).
Axes of the slice: x: 2, y: 2, z: 4, core: 2. Of those that a mesh axis runs over, the one named last changes fastest.
Arguments:
- psi: bfloat16 [8, 8, 3, 256, 256], P('row', None, None, 'col'), may hold values from -6 to 6
- left_ops: bfloat16 [8, 8, 32, 256, 256], P('row', None, 'col'), may hold values from -0.375 to 0.375
- right_ops: bfloat16 [8, 8, 32, 256, 256], P('row', None, 'col'), may hold values from -0.0625 to 0.0625
- mpo_pattern: int32 [8, 8, 32], P('row', None, 'col'), may hold values 0 or 1
- block_sizes: int32 [2, 8, 8], P(None, 'row'), may hold values from 1 to 256, 1280 in all within a row
Outputs:
- h_psi: bfloat16 [8, 8, 3, 256, 256], P('row', None, None, 'col')
Inputs may be any that keep to these rules, and one draw needn't show every extreme that they name: `block_sizes`: for each index and sector a, the 8 sizes along the last dimension sum to 1280.
All inputs are finite; a program needn't handle non-finite values. No bound on the sum of `mpo_pattern` on one device may be relied on, other than what follows from the above.
Results may differ from a plain program's by a relative error of at most 0.005.
Values may be sent and summed in bfloat16 or wider, within the bound.
A program may use at most 128 MiB of HBM per device.

v0:
```python
import jax
import jax.numpy as jnp
from jax import lax
from jax.sharding import PartitionSpec as P


def shards(psi, left_ops, right_ops, mpo_pattern, block_sizes):
    whole = lax.all_gather(psi, "col", axis=3, tiled=True)
    width = whole.shape[-1]
    index = jnp.arange(width, dtype=jnp.int32)
    live_rows = index < block_sizes[0][..., None]
    live_cols = index < block_sizes[1][..., None]
    keep = live_rows[:, :, None, :, None] & live_cols[:, :, None, None, :]
    live = jnp.where(keep, whole, jnp.zeros((), jnp.bfloat16))
    terms = jnp.einsum("abkrm,abvmc->abkvrc", left_ops, live, preferred_element_type=jnp.float32)
    terms = (terms * mpo_pattern[:, :, :, None, None, None].astype(jnp.float32)).astype(
        jnp.bfloat16
    )
    moved = lax.all_to_all(right_ops, "row", split_axis=1, concat_axis=0, tiled=True)
    partial_sum = jnp.einsum(
        "abkvrm,bakcm->abvrc", terms, moved, preferred_element_type=jnp.float32
    )
    result = lax.psum_scatter(partial_sum, "col", scatter_dimension=3, tiled=True).astype(
        jnp.bfloat16
    )
    height = result.shape[3]
    own_rows = lax.axis_index("col") * height + jnp.arange(height, dtype=jnp.int32)
    row_keep = own_rows < block_sizes[0][..., None]
    final_keep = row_keep[:, :, None, :, None] & live_cols[:, :, None, None, :]
    return jnp.where(final_keep, result, jnp.zeros((), jnp.bfloat16))


def solution(mesh):
    in_specs = (
        P("row", None, None, "col", None),
        P("row", None, "col", None, None),
        P("row", None, "col", None, None),
        P("row", None, "col"),
        P(None, "row", None),
    )
    out_specs = P("row", None, None, "col", None)
    return jax.shard_map(shards, mesh=mesh, in_specs=in_specs, out_specs=out_specs, check_vma=False)
```

profile of v0, /device:TPU:17, one launch (start us, length us, event | category | flops | bytes accessed | tf_op | source)
XLA Modules:
  0.0 284.0 jit_solution(1022732777311902965)
XLA Ops:
  6.5 0.0 copy-start.1
  6.5 0.0 copy-start
  6.5 5.7 %all-to-all-start = ((bf16[1,8,8,256,256]{4,3,2,0,1:T(8,128)(2,1)}), bf16[1,8,8,256,256]{4,3,2,0,1:T(8,128)(2,1)}, u32[]{:S(2)}, u32[]{:S(2)}) async-start(bf16[1,8,8,256,256]{4,3,2,0,1:T(8,128)(2,1)} %bitcast.54), calls=%async_computation | async-start | bytes 16777216 | tf_op jit(solution)/shard_map/all_to_all | solution.py:19
  12.2 0.0 all-gather.2.cloned.1.call-start
  12.3 0.7 all-gather.2.cloned.1.call-update
  13.0 0.0 reduce-scatter.2.cloned.1.call-start
  13.0 0.0 copy-done.1
  13.0 0.1 iota_compare_fusion
  13.1 0.0 copy-done
  13.1 0.5 broadcast_and_fusion
  13.6 31.5 %all-gather.2.cloned.1.call-done = bf16[1,8,3,256,256]{4,3,2,1,0:T(8,128)(2,1)} async-done(((bf16[1,8,3,64,256]{4,3,2,1,0:T(8,128)(2,1)}), bf16[1,8,3,256,256]{4,3,2,1,0:T(8,128)(2,1)}) %all-gather.2.cloned.1.call-update) | async-done | bytes 3145744 | tf_op jit(solution)/shard_map/all_gather | solution.py:8
  45.1 146.4 %all-to-all-done = bf16[1,8,8,256,256]{4,3,2,0,1:T(8,128)(2,1)} async-done(((bf16[1,8,8,256,256]{4,3,2,0,1:T(8,128)(2,1)}), bf16[1,8,8,256,256]{4,3,2,0,1:T(8,128)(2,1)}, u32[]{:S(2)}, u32[]{:S(2)}) %all-to-all-start) | async-done | bytes 8388640 | tf_op jit(solution)/shard_map/all_to_all | solution.py:19
  191.5 21.7 %fusion.16 = f32[1,8,3,256,256]{4,3,2,1,0:T(8,128)} fusion(bf16[1,8,8,256,256]{4,3,2,0,1:T(8,128)(2,1)} %all-to-all-done, f32[8,8]{1,0:T(8,128)S(1)} %convert_bitcast_fusion, bf16[1,8,8,256,256]{4,3,2,1,0:T(8,128)(2,1)} %param.6, bf16[1,8,3,256,256]{4,3,2,1,0:T(8,128)(2,1)} %all-gather.2.cloned.1.call-done, pred[8,256,256]{2,1,0:T(8,128)(4,1)S(1)} %broadcast_and_fusion), kind=kOutput, calls=%fused_computation.11 | convolution fusion | flops 12911640576 | bytes 26738944 | tf_op jit(solution)/shard_map/abkvrm,bakcm->abvrc/dot_general | solution.py:20
  213.2 0.0 reduce-scatter.2.cloned.1.call-update
  213.2 0.1 broadcast_compare_fusion
  213.3 0.1 broadcast_and_fusion.1
  213.4 61.4 %reduce-scatter.2.cloned.1.call-done = f32[1,8,3,64,256]{4,3,2,1,0:T(8,128)} async-done(((f32[1,8,3,256,256]{4,3,2,1,0:T(8,128)}), f32[1,8,3,64,256]{4,3,2,1,0:T(8,128)}) %reduce-scatter.2.cloned.1.call-update) | async-done | bytes 1572880 | tf_op jit(solution)/shard_map/reduce_scatter | solution.py:23
  274.8 2.4 convert_select_fusion
  (3 shorter events, 0.0 us)
Async XLA Ops:
  6.5 6.5 %copy-start.1 = (s32[2,1,8]{2,1,0:T(1,128)S(1)}, s32[2,1,8]{2,1,0:T(1,128)}, u32[]{:S(2)}) copy-start(s32[2,1,8]{2,1,0:T(1,128)} %param.9) | copy-start | bytes 196
  6.5 6.6 %copy-start = (s32[1,8,8]{2,1,0:T(8,128)S(1)}, s32[1,8,8]{2,1,0:T(8,128)}, u32[]{:S(2)}) copy-start(s32[1,8,8]{2,1,0:T(8,128)} %param.8) | copy-start | bytes 772
  6.5 184.9 %all-to-all-start = ((bf16[1,8,8,256,256]{4,3,2,0,1:T(8,128)(2,1)}), bf16[1,8,8,256,256]{4,3,2,0,1:T(8,128)(2,1)}, u32[]{:S(2)}, u32[]{:S(2)}) async-start(bf16[1,8,8,256,256]{4,3,2,0,1:T(8,128)(2,1)} %bitcast.54), calls=%async_computation | async-start | bytes 16777216 | tf_op jit(solution)/shard_map/all_to_all | solution.py:19
  12.2 32.8 %all-gather.2.cloned.1.call-start = ((), (), s32[]{:S(2)}) async-start(), calls=%async_computation.2 | async-start | bytes 3932160 | tf_op jit(solution)/shard_map/all_gather | solution.py:8
  13.0 261.9 %reduce-scatter.2.cloned.1.call-start = ((), (), s32[]{:S(2)}) async-start(), calls=%async_computation.3 | async-start | bytes 7864320 | tf_op jit(solution)/shard_map/reduce_scatter | solution.py:23
Sparse Core Ops, SparseCore 0:
  14.6 30.4 all-gather.1
  213.3 61.4 reduce-scatter.1
where the time goes:
time: 286 us; the launch traced here: 284 us
  waiting for transfers between devices  240 us (84%)
  matrix products  21.7 us (8%)
  between operations  13.4 us (5%)
  starting transfers between devices  5.75 us (2%)
  other arithmetic  3.14 us (1%)
    all_to_all x1, waiting for transfers between devices, shards(): lax.all_to_all(right_ops, 'row', split_axis=1, concat_axis=0, tiled=True)  146 us
    reduce_scatter x1, waiting for transfers between devices, shards(): lax.psum_scatter(partial_sum, 'col', scatter_dimension=3, tiled=True)  61.4 us
    all_gather x1, waiting for transfers between devices, shards(): whole = lax.all_gather(psi, 'col', axis=3, tiled=True)  31.5 us
    dot_general x1, matrix products, shards(): jnp.einsum('abkvrm,bakcm->abvrc', terms, moved, preferred_element_type=jn...  21.7 us
  transfers between devices with their start and end apart: 3, of which 3 were waited for; matrix products, arithmetic and copies ran while one was open for 0% of the time, Pallas kernels for 0%

commit v1 on v0

v1 whole, which is shorter than its diff:
```python
import functools

import jax
import jax.numpy as jnp
from jax import lax
from jax.experimental import pallas as pl
from jax.experimental.pallas import tpu as pltpu
from jax.sharding import PartitionSpec as P

MESH = pl.DeviceIdType.MESH
PARTS = 2


def partner(me, step, n):
    if n & (n - 1):
        return lax.rem(me + step, n)
    total, bit = 0, 1
    while bit < n:
        total = total + bit * (((me // bit) % 2 + (step // bit) % 2) % 2)
        bit *= 2
    return total


def source(me, step, n):
    if n & (n - 1):
        return lax.rem(me + n - step, n)
    return partner(me, step, n)


def kernel(
    n, nc, psi, left, right, pattern, sizes, out,
    whole, landed, lefts, live, terms, part, sums, own,
    psi_send, psi_recv, psi_own, right_send, right_recv, right_own, left_sem, sum_send, sum_recv,
):
    row, col = lax.axis_index("row"), lax.axis_index("col")
    channels, blk = left.shape[2], left.shape[3]
    vectors, height = psi.shape[2], psi.shape[3]
    width = blk // PARTS
    ahead = n // 2 + 1

    barrier = pltpu.get_barrier_semaphore()
    for step in range(1, n):
        pl.semaphore_signal(
            barrier, inc=1, device_id={"row": lax.rem(row + step, n)}, device_id_type=MESH
        )
    for step in range(1, nc):
        pl.semaphore_signal(
            barrier, inc=1, device_id={"col": lax.rem(col + step, nc)}, device_id_type=MESH
        )
    pl.semaphore_wait(barrier, n + nc - 2)

    def right_copy(step, p):
        to = partner(row, step, n)
        return pltpu.make_async_remote_copy(
            src_ref=right.at[0, to, :, pl.ds(p * width, width), :],
            dst_ref=landed.at[row, p],
            send_sem=right_send.at[step, p],
            recv_sem=right_recv.at[row, p],
            device_id={"row": to},
            device_id_type=MESH,
        )

    def right_arrival(step, p):
        b = source(row, step, n)
        return pltpu.make_async_remote_copy(
            src_ref=landed.at[b, p],
            dst_ref=landed.at[b, p],
            send_sem=right_send.at[step, p],
            recv_sem=right_recv.at[b, p],
            device_id={"row": b},
            device_id_type=MESH,
        )

    def right_local(p):
        return pltpu.make_async_copy(
            right.at[0, row, :, pl.ds(p * width, width), :], landed.at[row, p], right_own.at[p]
        )

    def psi_copy(off):
        return pltpu.make_async_remote_copy(
            src_ref=psi.at[0],
            dst_ref=whole.at[col],
            send_sem=psi_send.at[off],
            recv_sem=psi_recv.at[col],
            device_id={"col": lax.rem(col + off, nc)},
            device_id_type=MESH,
        )

    def psi_arrival(off):
        c = lax.rem(col + nc - off, nc)
        return pltpu.make_async_remote_copy(
            src_ref=psi.at[0],
            dst_ref=whole.at[c],
            send_sem=psi_send.at[off],
            recv_sem=psi_recv.at[c],
            device_id={"col": c},
            device_id_type=MESH,
        )

    def left_copy(step):
        return pltpu.make_async_copy(
            left.at[0, source(row, step, n)], lefts.at[step % 2], left_sem.at[step % 2]
        )

    def sum_copy(step, p, off):
        to = lax.rem(col + off, nc)
        b = source(row, step, n)
        return pltpu.make_async_remote_copy(
            src_ref=part.at[step % 2, p, to],
            dst_ref=sums.at[off - 1, b, p],
            send_sem=sum_send.at[off - 1, step % 2, p],
            recv_sem=sum_recv.at[off - 1, b, p],
            device_id={"col": to},
            device_id_type=MESH,
        )

    psi_local = pltpu.make_async_copy(psi.at[0], whole.at[col], psi_own)
    psi_local.start()
    left_copy(0).start()
    for p in range(PARTS):
        right_local(p).start()
    for off in range(1, nc):
        psi_copy(off).start()

    @pl.loop(1, min(ahead, n - 1) + 1)
    def _(step):
        for p in range(PARTS):
            right_copy(step, p).start()

    psi_local.wait()
    for off in range(1, nc):
        psi_arrival(off).wait_recv()

    def finish(step):
        b = source(row, step, n)
        live_rows, live_cols = sizes[0, 0, b], sizes[1, 0, b]
        r = lax.broadcasted_iota(jnp.int32, (height, width), 0) + col * height
        c = lax.broadcasted_iota(jnp.int32, (height, width), 1)
        for p in range(PARTS):
            for off in range(1, nc):
                sum_copy(step, p, off).wait_recv()
            keep = (r < live_rows) & (c + p * width < live_cols)
            for v in range(vectors):
                total = own[b, p, v]
                for off in range(1, nc):
                    total = total + sums[off - 1, b, p, v]
                out[0, b, v, :, p * width : (p + 1) * width] = jnp.where(keep, total, 0.0).astype(
                    out.dtype
                )

    @pl.loop(0, n)
    def _(step):
        b = source(row, step, n)

        @pl.when(step + 1 < n)
        def _():
            left_copy(step + 1).start()

        live_rows, live_cols = sizes[0, 0, b], sizes[1, 0, b]
        r = lax.broadcasted_iota(jnp.int32, (height, blk), 0)
        c = lax.broadcasted_iota(jnp.int32, (height, blk), 1)
        for g in range(nc):
            keep = (r + g * height < live_rows) & (c < live_cols)
            for v in range(vectors):
                block = whole[g, b, v].astype(jnp.float32)
                live[g * height : (g + 1) * height, v * blk : (v + 1) * blk] = jnp.where(
                    keep, block, 0.0
                ).astype(live.dtype)

        left_copy(step).wait()

        @pl.loop(0, channels)
        def _(k):
            acts = pattern[0, b, k].astype(jnp.float32)
            for v in range(vectors):
                term = jnp.dot(
                    lefts[step % 2, k],
                    live[:, v * blk : (v + 1) * blk],
                    preferred_element_type=jnp.float32,
                )
                terms[v, k] = (term * acts).astype(terms.dtype)

        for p in range(PARTS):

            @pl.when(step == 0)
            def _():
                right_local(p).wait()

            @pl.when(step > 0)
            def _():
                right_arrival(step, p).wait_recv()

            @pl.when(step >= 2)
            def _():
                for off in range(1, nc):
                    sum_copy(step - 2, p, off).wait_send()

            @pl.loop(0, vectors)
            def _(v):
                total = jnp.zeros((blk, width), jnp.float32)
                for k in range(channels):
                    total = total + lax.dot_general(
                        terms[v, k],
                        landed[b, p, k],
                        (((1,), (1,)), ((), ())),
                        preferred_element_type=jnp.float32,
                    )
                for g in range(nc):
                    part[step % 2, p, g, v] = total[g * height : (g + 1) * height]

            own[b, p] = part[step % 2, p, col]
            for off in range(1, nc):
                sum_copy(step, p, off).start()

        @pl.when((step >= ahead - 1) & (step + 2 < n))
        def _():
            for p in range(PARTS):
                right_copy(step + 2, p).start()

        @pl.when(step >= 1)
        def _():
            finish(step - 1)

    finish(n - 1)

    @pl.loop(1, n)
    def _(step):
        for p in range(PARTS):
            right_copy(step, p).wait_send()

    for off in range(1, nc):
        psi_copy(off).wait_send()
    for step in range(max(0, n - 2), n):
        for p in range(PARTS):
            for off in range(1, nc):
                sum_copy(step, p, off).wait_send()


def solution(mesh):
    n, nc = mesh.shape["row"], mesh.shape["col"]

    def shards(psi, left_ops, right_ops, mpo_pattern, block_sizes):
        _, nb, vectors, height, blk = psi.shape
        channels = left_ops.shape[2]
        width = blk // PARTS
        dma = pltpu.SemaphoreType.DMA
        flops = 4 * nb * channels * vectors * blk**3
        return pl.pallas_call(
            functools.partial(kernel, n, nc),
            out_shape=jax.ShapeDtypeStruct(psi.shape, jnp.bfloat16),
            in_specs=[pl.BlockSpec(memory_space=pl.ANY)] * 3
            + [pl.BlockSpec(memory_space=pltpu.SMEM)] * 2,
            out_specs=pl.BlockSpec(memory_space=pltpu.VMEM),
            scratch_shapes=[
                pltpu.VMEM((nc, nb, vectors, height, blk), jnp.bfloat16),
                pltpu.VMEM((nb, PARTS, channels, width, blk), jnp.bfloat16),
                pltpu.VMEM((2, channels, blk, blk), jnp.bfloat16),
                pltpu.VMEM((blk, vectors * blk), jnp.bfloat16),
                pltpu.VMEM((vectors, channels, blk, blk), jnp.bfloat16),
                pltpu.VMEM((2, PARTS, nc, vectors, height, width), jnp.float32),
                pltpu.VMEM((nc - 1, nb, PARTS, vectors, height, width), jnp.float32),
                pltpu.VMEM((nb, PARTS, vectors, height, width), jnp.float32),
                dma((nc,)),
                dma((nc,)),
                dma,
                dma((n, PARTS)),
                dma((n, PARTS)),
                dma((PARTS,)),
                dma((2,)),
                dma((nc - 1, 2, PARTS)),
                dma((nc - 1, nb, PARTS)),
            ],
            compiler_params=pltpu.CompilerParams(
                collective_id=0, has_side_effects=True, vmem_limit_bytes=56 * 2**20
            ),
            cost_estimate=pl.CostEstimate(
                flops=flops, bytes_accessed=4 * left_ops.size, transcendentals=0
            ),
        )(psi, left_ops, right_ops, mpo_pattern, block_sizes)

    in_specs = (
        P("row", None, None, "col", None),
        P("row", None, "col", None, None),
        P("row", None, "col", None, None),
        P("row", None, "col"),
        P(None, "row", None),
    )
    out_specs = P("row", None, None, "col", None)
    return jax.shard_map(shards, mesh=mesh, in_specs=in_specs, out_specs=out_specs, check_vma=False)
```

time: 286 us -> 198 us (0.69)
  waiting for transfers between devices: 240 us -> 0 us
  Pallas kernels: 0 us -> 196 us
  matrix products: 21.7 us -> 0 us
  between operations: 13.4 us -> 0.01 us
  starting transfers between devices: 5.75 us -> 0 us
  other arithmetic: 3.14 us -> 0 us
    pallas_call x0 -> x1, Pallas kernels: none -> 196 us  [shards(): pl.pallas_call(functools.partial(kernel, n, nc), out_shape=jax.ShapeDtype...]
    all_to_all x1 -> x0, waiting for transfers between devices: 146 us -> none  [shards(): lax.all_to_all(right_ops, 'row', split_axis=1, concat_axis=0, tiled=True)]
    reduce_scatter x1 -> x0, waiting for transfers between devices: 61.4 us -> none  [shards(): lax.psum_scatter(partial_sum, 'col', scatter_dimension=3, tiled=True)]
    all_gather x1 -> x0, waiting for transfers between devices: 31.5 us -> none  [shards(): whole = lax.all_gather(psi, 'col', axis=3, tiled=True)]
    dot_general x1 -> x0, matrix products: 21.7 us -> none  [shards(): jnp.einsum('abkvrm,bakcm->abvrc', terms, moved, preferred_element_type=jn...]
    all_to_all x1 -> x0, starting transfers between devices: 5.71 us -> none  [shards(): lax.all_to_all(right_ops, 'row', split_axis=1, concat_axis=0, tiled=True)]
  transfers between devices with their start and end apart: 3 -> 0, of which waited for: 3 -> 0; matrix products, arithmetic and copies ran while one was open for 0% -> 0% of each run, Pallas kernels for 0% -> 0%
where the time goes in v1:
time: 198 us
  Pallas kernels  196 us (99%)
  local copies, waits for them, and re-layouts  2.09 us (1%)
    pallas_call x1, Pallas kernels, shards(): pl.pallas_call(functools.partial(kernel, n, nc), out_shape=jax.ShapeDtype...  196 us

profile of v1, /device:TPU:17, one launch (start us, length us, event | category | flops | bytes accessed | tf_op | source)
XLA Modules:
  0.0 197.9 jit_solution(12549725013161447962)
XLA Ops:
  0.0 195.8 %shard_map.55 = bf16[1,8,3,64,256]{4,3,2,1,0:T(8,128)(2,1)} custom-call(bf16[1,8,3,64,256]{4,3,2,1,0:T(8,128)(2,1)} %psi.1, bf16[1,8,8,256,256]{4,3,2,1,0:T(8,128)(2,1)} %left.1, bf16[1,8,8,256,256]{4,3,2,1,0:T(8,128)(2,1)} %right.1, s32[1,8,8]{2,1,0:T(8,128)} %pattern.1, s32[2,1,8]{2,1,0:T(1,128)} %sizes.1), custom_call_target="tpu_custom_call" | custom-call | flops 12884901888 | bytes 16777216 | tf_op jit(solution)/shard_map/pallas_call | solution.py:248
  195.8 2.1 %copy.7 = bf16[1,8,3,64,256]{4,3,2,1,0:T(8,128)(2,1)} copy(bf16[1,8,3,64,256]{4,3,2,1,0:T(8,128)(2,1)} %shard_map.55) | data formatting | bytes 1572864

commit v2 on v1

--- a/solution.py
+++ b/solution.py
@@ -9,6 +9,7 @@
 
 MESH = pl.DeviceIdType.MESH
 PARTS = 2
+FLIGHT = 3
 
 
 def partner(me, step, n):
@@ -36,7 +37,7 @@
     channels, blk = left.shape[2], left.shape[3]
     vectors, height = psi.shape[2], psi.shape[3]
     width = blk // PARTS
-    ahead = n // 2 + 1
+    far = n // 2
 
     barrier = pltpu.get_barrier_semaphore()
     for step in range(1, n):
@@ -47,7 +48,6 @@
         pl.semaphore_signal(
             barrier, inc=1, device_id={"col": lax.rem(col + step, nc)}, device_id_type=MESH
         )
-    pl.semaphore_wait(barrier, n + nc - 2)
 
     def right_copy(step, p):
         to = partner(row, step, n)
@@ -102,14 +102,14 @@
             left.at[0, source(row, step, n)], lefts.at[step % 2], left_sem.at[step % 2]
         )
 
-    def sum_copy(step, p, off):
+    def sum_copy(step, p, v, off):
         to = lax.rem(col + off, nc)
         b = source(row, step, n)
         return pltpu.make_async_remote_copy(
-            src_ref=part.at[step % 2, p, to],
-            dst_ref=sums.at[off - 1, b, p],
-            send_sem=sum_send.at[off - 1, step % 2, p],
-            recv_sem=sum_recv.at[off - 1, b, p],
+            src_ref=part.at[step % 2, p, to, v],
+            dst_ref=sums.at[off - 1, b, p, v],
+            send_sem=sum_send.at[off - 1, step % 2, p, v],
+            recv_sem=sum_recv.at[off - 1, b, p, v],
             device_id={"col": to},
             device_id_type=MESH,
         )
@@ -119,13 +119,17 @@
     left_copy(0).start()
     for p in range(PARTS):
         right_local(p).start()
+    pl.semaphore_wait(barrier, n + nc - 2)
     for off in range(1, nc):
         psi_copy(off).start()
 
-    @pl.loop(1, min(ahead, n - 1) + 1)
-    def _(step):
-        for p in range(PARTS):
-            right_copy(step, p).start()
+    far_span, near_span = (far, min(far + FLIGHT, n)), (1, far)
+    for span in (near_span, far_span):
+
+        @pl.loop(*span)
+        def _(step):
+            for p in range(PARTS):
+                right_copy(step, p).start()
 
     psi_local.wait()
     for off in range(1, nc):
@@ -137,10 +141,10 @@
         r = lax.broadcasted_iota(jnp.int32, (height, width), 0) + col * height
         c = lax.broadcasted_iota(jnp.int32, (height, width), 1)
         for p in range(PARTS):
-            for off in range(1, nc):
-                sum_copy(step, p, off).wait_recv()
             keep = (r < live_rows) & (c + p * width < live_cols)
             for v in range(vectors):
+                for off in range(1, nc):
+                    sum_copy(step, p, v, off).wait_recv()
                 total = own[b, p, v]
                 for off in range(1, nc):
                     total = total + sums[off - 1, b, p, v]
@@ -190,10 +194,15 @@
             def _():
                 right_arrival(step, p).wait_recv()
 
+            @pl.when((step >= far) & (step + FLIGHT < n))
+            def _():
+                right_copy(step + FLIGHT, p).start()
+
             @pl.when(step >= 2)
             def _():
-                for off in range(1, nc):
-                    sum_copy(step - 2, p, off).wait_send()
+                for v in range(vectors):
+                    for off in range(1, nc):
+                        sum_copy(step - 2, p, v, off).wait_send()
 
             @pl.loop(0, vectors)
             def _(v):
@@ -207,15 +216,9 @@
                     )
                 for g in range(nc):
                     part[step % 2, p, g, v] = total[g * height : (g + 1) * height]
-
-            own[b, p] = part[step % 2, p, col]
-            for off in range(1, nc):
-                sum_copy(step, p, off).start()
-
-        @pl.when((step >= ahead - 1) & (step + 2 < n))
-        def _():
-            for p in range(PARTS):
-                right_copy(step + 2, p).start()
+                for off in range(1, nc):
+                    sum_copy(step, p, v, off).start()
+                own[b, p, v] = part[step % 2, p, col, v]
 
         @pl.when(step >= 1)
         def _():
@@ -232,8 +235,9 @@
         psi_copy(off).wait_send()
     for step in range(max(0, n - 2), n):
         for p in range(PARTS):
-            for off in range(1, nc):
-                sum_copy(step, p, off).wait_send()
+            for v in range(vectors):
+                for off in range(1, nc):
+                    sum_copy(step, p, v, off).wait_send()
 
 
 def solution(mesh):
@@ -267,8 +271,8 @@
                 dma((n, PARTS)),
                 dma((PARTS,)),
                 dma((2,)),
-                dma((nc - 1, 2, PARTS)),
-                dma((nc - 1, nb, PARTS)),
+                dma((nc - 1, 2, PARTS, vectors)),
+                dma((nc - 1, nb, PARTS, vectors)),
             ],
             compiler_params=pltpu.CompilerParams(
                 collective_id=0, has_side_effects=True, vmem_limit_bytes=56 * 2**20

time: 198 us -> 197 us (level)
  Pallas kernels: 196 us -> 194 us
where the time goes in v2:
time: 197 us; the launch traced here: 196 us
  Pallas kernels  194 us (98%)
  local copies, waits for them, and re-layouts  2.09 us (1%)
    pallas_call x1, Pallas kernels, shards(): pl.pallas_call(functools.partial(kernel, n, nc), out_shape=jax.ShapeDtype...  194 us

profile of v2, /device:TPU:17, one launch (start us, length us, event | category | flops | bytes accessed | tf_op | source)
XLA Modules:
  0.0 196.3 jit_solution(7778731853854863578)
XLA Ops:
  0.0 194.2 %shard_map.55 = bf16[1,8,3,64,256]{4,3,2,1,0:T(8,128)(2,1)} custom-call(bf16[1,8,3,64,256]{4,3,2,1,0:T(8,128)(2,1)} %psi.1, bf16[1,8,8,256,256]{4,3,2,1,0:T(8,128)(2,1)} %left.1, bf16[1,8,8,256,256]{4,3,2,1,0:T(8,128)(2,1)} %right.1, s32[1,8,8]{2,1,0:T(8,128)} %pattern.1, s32[2,1,8]{2,1,0:T(1,128)} %sizes.1), custom_call_target="tpu_custom_call" | custom-call | flops 12884901888 | bytes 16777216 | tf_op jit(solution)/shard_map/pallas_call | solution.py:252
  194.2 2.1 %copy.7 = bf16[1,8,3,64,256]{4,3,2,1,0:T(8,128)(2,1)} copy(bf16[1,8,3,64,256]{4,3,2,1,0:T(8,128)(2,1)} %shard_map.55) | data formatting | bytes 1572864

commit v3 on v2

--- a/solution.py
+++ b/solution.py
@@ -120,17 +120,17 @@
     for p in range(PARTS):
         right_local(p).start()
     pl.semaphore_wait(barrier, n + nc - 2)
-    for off in range(1, nc):
-        psi_copy(off).start()
 
     far_span, near_span = (far, min(far + FLIGHT, n)), (1, far)
-    for span in (near_span, far_span):
+    for span in (far_span, near_span):
 
         @pl.loop(*span)
         def _(step):
             for p in range(PARTS):
                 right_copy(step, p).start()
 
+    for off in range(1, nc):
+        psi_copy(off).start()
     psi_local.wait()
     for off in range(1, nc):
         psi_arrival(off).wait_recv()

time: 197 us -> 198 us (level)
  no operation moved by 1% of the time
where the time goes in v3:
time: 198 us; the launch traced here: 196 us
  Pallas kernels  194 us (98%)
  local copies, waits for them, and re-layouts  2.09 us (1%)
    pallas_call x1, Pallas kernels, shards(): pl.pallas_call(functools.partial(kernel, n, nc), out_shape=jax.ShapeDtype...  194 us

profile of v3, /device:TPU:17, one launch (start us, length us, event | category | flops | bytes accessed | tf_op | source)
XLA Modules:
  0.0 196.4 jit_solution(11394427670704032693)
XLA Ops:
  0.0 194.3 %shard_map.55 = bf16[1,8,3,64,256]{4,3,2,1,0:T(8,128)(2,1)} custom-call(bf16[1,8,3,64,256]{4,3,2,1,0:T(8,128)(2,1)} %psi.1, bf16[1,8,8,256,256]{4,3,2,1,0:T(8,128)(2,1)} %left.1, bf16[1,8,8,256,256]{4,3,2,1,0:T(8,128)(2,1)} %right.1, s32[1,8,8]{2,1,0:T(8,128)} %pattern.1, s32[2,1,8]{2,1,0:T(1,128)} %sizes.1), custom_call_target="tpu_custom_call" | custom-call | flops 12884901888 | bytes 16777216 | tf_op jit(solution)/shard_map/pallas_call | solution.py:252
  194.3 2.1 %copy.7 = bf16[1,8,3,64,256]{4,3,2,1,0:T(8,128)(2,1)} copy(bf16[1,8,3,64,256]{4,3,2,1,0:T(8,128)(2,1)} %shard_map.55) | data formatting | bytes 1572864
